TPU v7x, 256 devices: a whole 4x4x8 slice. The times are simulated.
256 devices in a mesh: ctx: 16 (over y, x_lo, core), head: 8 (over z), grp: 2 (over x_hi).
Axes of the slice: x: 4 (x_hi: 2, x_lo: 2; x = x_hi * 2 + x_lo), y: 4, z: 8, core: 2. Of those that a mesh axis runs over, the one named last changes fastest.
Arguments:
- queries: bfloat16 [8192, 8192], P(('ctx', 'grp'), 'head'), may hold values from -18 to 18
- answer_kv: bfloat16 [8192, 8, 256], P(('ctx', 'grp'), 'head'), may hold values from -8 to 8
- prompt_kv: bfloat16 [2, 8192, 8, 256], P('grp', 'ctx', 'head'), may hold values from -8 to 8
- block_prompt: int32 [64, 1], P(('ctx', 'grp')), may hold values from 0 to 1; in each aligned block of 2 rows (0 to 1, 2 to 3, ...) at most 2 rows name the same one
- answer_len: int32 [64], P(('ctx', 'grp')), may hold values from 1 to 128, 5120 in all
Outputs:
- attended: bfloat16 [8192, 8192], P(('ctx', 'grp'), 'head')
Inputs may be any that keep to these rules, and one draw needn't show every extreme that they name: `block_prompt`: of the 2 blocks that one index of ctx and grp holds (aligned blocks of rows), at most 2 name any one prompt.
All inputs are finite; a program needn't handle non-finite values. No bound on the sum of `answer_len` on one device may be relied on, other than what follows from the above.
Results may differ from a plain program's by a relative error of at most 0.0055.
Values may be sent and summed in bfloat16 or wider, within the bound.
No kernel may reach another device: no remote copies, remote signals or barrier semaphores. Data moves between devices by JAX's collectives and lax.ppermute only.
A program may use at most 256 MiB of HBM per device.

v0:
```python
import functools

import jax
import jax.numpy as jnp
import numpy as np
from jax import lax
from jax.experimental import pallas as pl
from jax.experimental.pallas import tpu as pltpu
from jax.sharding import PartitionSpec as P

HD = 128
BROWS = 128
HEADS = 8
BLOCK = 1024
GROUP = 16
TILE = 4
LIST = 8
SPARE = 32
STATE_ROWS = 33 * GROUP * HEADS
SCALE = float(np.log2(np.e) / np.sqrt(HD))
LOW = -1e30
VMEM = pl.BlockSpec(memory_space=pltpu.VMEM)
SMEM = pl.BlockSpec(memory_space=pltpu.SMEM)
AXES = ("ctx", "grp")

TURNS = {"even": lambda i: i ^ 1, "odd": lambda i: 3 - i, "across": lambda i: i ^ 2}


def index_of(x, y, core):
    return ((y * 2 + x % 2) * 2 + core) * 2 + x // 2


def ring_swap(stage, turn):
    pairs = []
    for x in range(4):
        for y in range(4):
            for core in range(2):
                to = (TURNS[turn](x), y) if core == stage else (x, TURNS[turn](y))
                pairs.append((index_of(x, y, core), index_of(*to, core)))
    return pairs


def core_swap():
    return [(index_of(x, y, c), index_of(x, y, 1 - c)) for x in range(4) for y in range(4) for c in range(2)]


def scaled(q):
    wide = q.astype(jnp.float32) * SCALE
    high = wide.astype(jnp.bfloat16)
    low = (wide - high.astype(jnp.float32)).astype(jnp.bfloat16)
    return jnp.concatenate([high, low], axis=1)


def scores_of(q, k):
    return lax.dot_general(
        q, jnp.concatenate([k, k], axis=1), (((1,), (1,)), ((), ())), preferred_element_type=jnp.float32
    )


def with_ones(v):
    return jnp.concatenate([v, jnp.ones_like(v)], axis=1)


def put_stats(lane, stats, h, m, l):
    stats = jnp.where(lane == h, m, stats)
    return jnp.where(lane == HEADS + h, l, stats)


def make_plan(meta_ref, plan_ref):
    offset = jnp.int32(0)
    for want in range(2):
        count = jnp.int32(0)
        for b in range(4):
            code = meta_ref[b]
            live = ((code & 255) + (GROUP - 1)) // GROUP
            live = jnp.where((code >> 8) == (meta_ref[4] ^ want), live, 0)

            def add(i, c, b=b, at=LIST + offset + count):
                plan_ref[at + i] = b * 8 + i
                return c

            lax.fori_loop(0, live, add, 0)
            count = count + live
        tiles = (count + (TILE - 1)) // TILE
        for i in range(TILE - 1):
            plan_ref[LIST + offset + count + i] = SPARE
        plan_ref[want] = tiles
        offset = offset + tiles * TILE
    plan_ref[2] = meta_ref[5]


def rows_of(group):
    return pl.ds(pl.multiple_of(group * (GROUP * HEADS), GROUP * HEADS), GROUP * HEADS)


def prep_kernel(meta_ref, q_ref, far_ref, kv_ref, plan_ref, qs_ref, m_ref, l_ref, a_ref):
    make_plan(meta_ref, plan_ref)
    shape = (HEADS * BROWS, BROWS)
    row = lax.broadcasted_iota(jnp.int32, shape, 0) % BROWS
    causal = row >= lax.broadcasted_iota(jnp.int32, shape, 1)
    for b in range(2):
        rows = slice(b * BROWS, (b + 1) * BROWS)
        q = scaled(jnp.concatenate([q_ref[rows, h * HD : (h + 1) * HD] for h in range(HEADS)], axis=0))
        s = jnp.where(causal, scores_of(q, kv_ref[rows, 0:HD]), LOW)
        m = jnp.max(s, axis=1, keepdims=True)
        p = jnp.exp2(s - m)
        pv = jnp.dot(p.astype(jnp.bfloat16), with_ones(kv_ref[rows, HD:]), preferred_element_type=jnp.float32)
        m = jnp.broadcast_to(m, (HEADS * BROWS, HD))
        for g in range(8):
            for h in range(HEADS):
                here = slice(((b * 8 + g) * HEADS + h) * GROUP, ((b * 8 + g) * HEADS + h + 1) * GROUP)
                part = slice(h * BROWS + g * GROUP, h * BROWS + (g + 1) * GROUP)
                qs_ref[here, :] = q[part]
                m_ref[here, :] = m[part]
                l_ref[here, :] = pv[part, HD:]
                a_ref[here, :] = pv[part, :HD]
    for g in range(16):
        for h in range(HEADS):
            here = slice(((16 + g) * HEADS + h) * GROUP, ((16 + g) * HEADS + h + 1) * GROUP)
            qs_ref[here, :] = scaled(far_ref[g * GROUP : (g + 1) * GROUP, h * HD : (h + 1) * HD])
    rest = slice(16 * GROUP * HEADS, STATE_ROWS)
    size = (STATE_ROWS - 16 * GROUP * HEADS, HD)
    m_ref[rest, :] = jnp.full(size, LOW, jnp.float32)
    l_ref[rest, :] = jnp.zeros(size, jnp.float32)
    a_ref[rest, :] = jnp.zeros(size, jnp.float32)
    qs_ref[SPARE * GROUP * HEADS : STATE_ROWS, :] = jnp.zeros((GROUP * HEADS, 2 * HD), jnp.bfloat16)


def prep(meta, q, far, kv):
    return pl.pallas_call(
        prep_kernel,
        out_shape=[
            jax.ShapeDtypeStruct((64,), jnp.int32),
            jax.ShapeDtypeStruct((STATE_ROWS, 2 * HD), jnp.bfloat16),
        ]
        + [jax.ShapeDtypeStruct((STATE_ROWS, HD), jnp.float32)] * 3,
        in_specs=[SMEM] + [VMEM] * 3,
        out_specs=[SMEM] + [VMEM] * 4,
        compiler_params=pltpu.CompilerParams(vmem_limit_bytes=40 * 2**20),
        cost_estimate=pl.CostEstimate(flops=2 * 2048 * 128 * 512, bytes_accessed=3 * 2**20, transcendentals=2048 * 128),
        name="prep",
    )(meta, q, far, kv)


def fold_kernel(number, *refs):
    refs = list(refs)
    plan_ref, qs_ref, kv_ref = refs[:3]
    m_ref, l_ref, a_ref = refs[6:9]
    item_at, item_kv, s0_ref, s1_ref = refs[-4:]
    core = plan_ref[2]

    items, first = jnp.int32(0), jnp.int32(LIST)
    for want in range(2):
        tiles = plan_ref[want]
        if number == 1:
            blocks, many = (want, 0), 1
        elif number == 2:
            blocks, many = (want ^ core, 0), 1
        else:
            blocks = (jnp.where(core == 0, want, 0), 1)
            many = jnp.where(core == 0, 1, 2 if (want == 0) == (number == 0) else 0)

        def add(t, c, first=first, blocks=blocks, many=many, items=items):
            for i in range(1 if number in (1, 2) else 2):

                @pl.when(i < many)
                def _(i=i):
                    item_at[items + t * many + i] = first + t * TILE
                    item_kv[items + t * many + i] = blocks[i]

            return c

        lax.fori_loop(0, tiles, add, 0)
        items = items + tiles * many
        first = first + tiles * TILE
    for i in range(2):
        item_at[items + i] = LIST
        item_kv[items + i] = 0

    def tile(i):
        return [rows_of(plan_ref[item_at[i] + g]) for g in range(TILE)]

    def positions(i):
        return pl.ds(pl.multiple_of(item_kv[i] * BLOCK, BLOCK), BLOCK)

    def load(ref, rows):
        return jnp.concatenate([ref[r, :] for r in rows], axis=0)

    def save(ref, rows, value):
        for g, r in enumerate(rows):
            ref[r, :] = value[g * GROUP * HEADS : (g + 1) * GROUP * HEADS]

    def score(i, s_ref):
        s_ref[...] = scores_of(load(qs_ref, tile(i)), kv_ref[positions(i), 0:HD])

    def soften(i, s_ref):
        here = tile(i)
        s, m = s_ref[...], load(m_ref, here)
        fresh = jnp.maximum(m, jnp.max(s, axis=1, keepdims=True))
        shrink = jnp.exp2(m - fresh)
        p = jnp.exp2(s - jnp.concatenate([fresh] * (BLOCK // HD), axis=1)).astype(jnp.bfloat16)
        pv = jnp.dot(p, with_ones(kv_ref[positions(i), HD:]), preferred_element_type=jnp.float32)
        save(m_ref, here, fresh)
        save(l_ref, here, load(l_ref, here) * shrink + pv[:, HD:])
        save(a_ref, here, load(a_ref, here) * shrink + pv[:, :HD])

    @pl.when(items > 0)
    def _():
        score(0, s0_ref)

    def pair(j, c):
        i = j * 2
        score(i + 1, s1_ref)
        soften(i, s0_ref)
        score(i + 2, s0_ref)
        soften(i + 1, s1_ref)
        return c

    lax.fori_loop(0, items // 2, pair, 0)

    @pl.when(items % 2 == 1)
    def _():
        soften(items - 1, s0_ref)

    if number == 3:
        far_ref, far_stat_ref = refs[9:11]
        lane = lax.broadcasted_iota(jnp.int32, (GROUP, 128), 1)
        for g in range(16):
            to = slice(g * GROUP, (g + 1) * GROUP)
            stats = jnp.zeros((GROUP, 128), jnp.float32)
            for h in range(HEADS):
                here = slice(((16 + g) * HEADS + h) * GROUP, ((16 + g) * HEADS + h + 1) * GROUP)
                stats = put_stats(lane, stats, h, m_ref[here, :], l_ref[here, :])
                far_ref[to, h * HD : (h + 1) * HD] = a_ref[here, :].astype(jnp.bfloat16)
            far_stat_ref[to, :] = stats


def fold_call(number, plan, qs, kv, state):
    f32, b16 = jnp.float32, jnp.bfloat16
    shapes = [((STATE_ROWS, HD), f32)] * 3
    if number == 3:
        shapes += [((256, 1024), b16), ((256, 128), f32)]
    operands = [plan, qs, kv, *state]
    wide = (TILE * GROUP * HEADS, BLOCK)
    return pl.pallas_call(
        functools.partial(fold_kernel, number),
        out_shape=[jax.ShapeDtypeStruct(s, d) for s, d in shapes],
        in_specs=[SMEM] + [VMEM] * (len(operands) - 1),
        out_specs=[VMEM] * len(shapes),
        scratch_shapes=[pltpu.SMEM((48,), jnp.int32)] * 2 + [pltpu.VMEM(wide, f32)] * 2,
        input_output_aliases={3: 0, 4: 1, 5: 2},
        compiler_params=pltpu.CompilerParams(vmem_limit_bytes=40 * 2**20),
        cost_estimate=pl.CostEstimate(
            flops=2 * 2560 * kv.shape[0] * 256, bytes_accessed=4 * 2**20, transcendentals=1280 * kv.shape[0]
        ),
        name=f"fold{number}",
    )(*operands)


def join_kernel(len_ref, m_ref, l_ref, a_ref, far_ref, far_stat_ref, out_ref):
    for b in range(2):
        for part in range(2):
            length = len_ref[b] - part * 4 * GROUP
            first = b * BROWS + part * 4 * GROUP

            @pl.when(length > 0)
            def _(b=b, part=part, length=length, first=first):
                for g in range(4):
                    group = b * 8 + part * 4 + g
                    rows = slice(group * GROUP, (group + 1) * GROUP)
                    live = lax.broadcasted_iota(jnp.int32, (GROUP, HD), 0) < length - g * GROUP
                    stats = far_stat_ref[rows, :]
                    for h in range(HEADS):
                        cols = slice(h * HD, (h + 1) * HD)
                        here = slice((group * HEADS + h) * GROUP, (group * HEADS + h + 1) * GROUP)
                        m, far_m = m_ref[here, :], stats[:, h : h + 1]
                        peak = jnp.maximum(m, far_m)
                        w, far_w = jnp.exp2(m - peak), jnp.exp2(far_m - peak)
                        total = w * l_ref[here, :] + far_w * stats[:, HEADS + h : HEADS + h + 1]
                        blended = w * a_ref[here, :] + far_w * far_ref[rows, cols].astype(jnp.float32)
                        out_ref[rows, cols] = jnp.where(live, blended / total, 0.0).astype(jnp.bfloat16)

            @pl.when(length <= 0)
            def _(first=first):
                out_ref[first : first + 4 * GROUP, :] = jnp.zeros((4 * GROUP, HEADS * HD), jnp.bfloat16)


def join(lengths, state, far, far_stat):
    return pl.pallas_call(
        join_kernel,
        out_shape=jax.ShapeDtypeStruct((256, 1024), jnp.bfloat16),
        in_specs=[SMEM] + [VMEM] * 5,
        out_specs=VMEM,
        compiler_params=pltpu.CompilerParams(vmem_limit_bytes=32 * 2**20),
        name="join",
    )(lengths, *state, far, far_stat)


def per_device(queries, answer_kv, prompt_kv, block_prompt, answer_len):
    piece = prompt_kv[0, :, 0, :]
    own_kv = answer_kv[:, 0, :]
    code = block_prompt[:, 0] * 256 + answer_len
    place = jnp.stack([lax.axis_index("grp"), lax.axis_index("ctx") & 1]).astype(jnp.int32)

    even, odd, across = [lax.ppermute(piece, AXES, ring_swap(0, turn)) for turn in ("even", "odd", "across")]
    code_far, q_far = [lax.ppermute(v, AXES, core_swap()) for v in (code, queries)]
    room = jnp.pad(piece, ((0, piece.shape[0]), (0, 0)))
    plan, qs, *state = prep(jnp.concatenate([code, code_far, place]), queries, q_far, own_kv)
    even, odd, across, room, plan, qs, state = lax.optimization_barrier((even, odd, across, room, plan, qs, state))
    held = [lax.dynamic_update_slice(room, even, (piece.shape[0], 0)), jnp.concatenate([odd, across], axis=0)]
    even0, even1 = [lax.ppermute(h, AXES, ring_swap(1, "even")) for h in held]
    odd0, odd1 = [lax.ppermute(h, AXES, ring_swap(1, "odd")) for h in held]
    all_held = jnp.concatenate(held, axis=0)
    across = lax.ppermute(all_held, AXES, ring_swap(1, "across"))
    state = fold_call(0, plan, qs, all_held, state)
    even0, odd1, state = lax.optimization_barrier((even0, odd1, state))
    state = fold_call(1, plan, qs, jnp.concatenate([even0, odd1], axis=0), state)
    odd0, even1, state = lax.optimization_barrier((odd0, even1, state))
    state = fold_call(2, plan, qs, jnp.concatenate([odd0, even1], axis=0), state)
    across, state = lax.optimization_barrier((across, state))
    *state, far, far_stat = fold_call(3, plan, qs, across, state)
    far = lax.ppermute(far, AXES, core_swap())
    far_stat = lax.ppermute(far_stat, AXES, core_swap())
    return join(answer_len, state, far, far_stat)


def solution(mesh):
    placed = (
        P(("ctx", "grp"), "head"),
        P(("ctx", "grp"), "head", None),
        P("grp", "ctx", "head", None),
        P(("ctx", "grp"), None),
        P(("ctx", "grp")),
    )
    return jax.shard_map(
        per_device, mesh=mesh, in_specs=placed, out_specs=P(("ctx", "grp"), "head"), check_vma=False
    )
```

profile of v0, /device:TPU:141, one launch (start us, length us, event | category | flops | bytes accessed | tf_op | source)
XLA Modules:
  0.0 54.2 jit_solution(15327518797545701129)
XLA Ops:
  0.0 0.7 %collective-permute-start.4 = (bf16[256,1024]{1,0:T(8,128)(2,1)}, bf16[256,1024]{1,0:T(8,128)(2,1)S(1)}, u32[]{:S(2)}, u32[]{:S(2)}) collective-permute-start(bf16[256,1024]{1,0:T(8,128)(2,1)} %q_ref.1), channel_id=1, source_target_pairs={{0,16},{16,0},{64,80},{80,64},{128,144},{144,128},{192,208},{208,1... | collective-permute-start | bytes 1572872 | tf_op jit(solution)/shard_map/ppermute | solution.py:306
  0.7 2.0 %collective-permute-start.2 = (bf16[512,256]{1,0:T(8,128)(2,1)}, bf16[512,256]{1,0:T(8,128)(2,1)S(1)}, u32[]{:S(2)}, u32[]{:S(2)}) collective-permute-start(bf16[512,256]{1,0:T(8,128)(2,1)} %bitcast.7), channel_id=1, source_target_pairs={{0,1},{16,144},{64,65},{80,208},{128,129},{144,16},{192,193},{208,... | collective-permute-start | bytes 786440 | tf_op jit(solution)/shard_map/ppermute | solution.py:305
  2.7 0.0 collective-permute-start.1
  2.7 1.8 %collective-permute-start = (bf16[512,256]{1,0:T(8,128)(2,1)}, bf16[512,256]{1,0:T(8,128)(2,1)S(1)}, u32[]{:S(2)}, u32[]{:S(2)}) collective-permute-start(bf16[512,256]{1,0:T(8,128)(2,1)} %bitcast.9), channel_id=1, source_target_pairs={{0,32},{16,80},{64,96},{80,16},{128,160},{144,208},{192,224},{208,... | collective-permute-start | bytes 786440 | tf_op jit(solution)/shard_map/ppermute | solution.py:305
  4.5 0.7 %bitcast_add_fusion = s32[2]{0:T(128)S(1)} fusion(s32[2]{0:T(128)} %len_ref.1, s32[2,1]{0,1:T(1,128)} %param.8), kind=kLoop, calls=%fused_computation.6 | loop fusion | flops 4 | bytes 24 | tf_op jit(solution)/shard_map/add | solution.py:302
  5.2 0.8 %collective-permute-start.3 = (s32[2]{0:T(128)S(1)}, s32[2]{0:T(128)S(1)}, u32[]{:S(2)}, u32[]{:S(2)}) collective-permute-start(s32[2]{0:T(128)S(1)} %bitcast_add_fusion), channel_id=1, source_target_pairs={{0,16},{16,0},{64,80},{80,64},{128,144},{144,128},{192,208},{208,1... | collective-permute-start | bytes 32 | tf_op jit(solution)/shard_map/ppermute | solution.py:306
  6.1 1.0 %pad.4 = bf16[1024,256]{1,0:T(8,128)(2,1)S(1)} pad(bf16[512,256]{1,0:T(8,128)(2,1)} %bitcast.10, bf16[]{:T(256)} %constant.4.clone.1), padding=0_512x0_0 | pad | bytes 786434 | tf_op jit(solution)/shard_map/jit(_pad)/pad | solution.py:307
  7.0 0.0 collective-permute-done.3
  7.1 0.1 pad_add_fusion.meta_ref
  7.1 0.0 collective-permute-done.4.far_ref
  7.1 0.0 copy-start
  7.1 1.0 %copy-done = bf16[256,1024]{1,0:T(8,128)(2,1)S(1)} copy-done((bf16[256,1024]{1,0:T(8,128)(2,1)S(1)}, bf16[256,1024]{1,0:T(8,128)(2,1)}, u32[]{:S(2)}) %copy-start) | copy-done | bytes 524312
  8.2 0.0 copy-start.1
  8.2 0.9 %copy-done.1 = bf16[256,1,256]{2,0,1:T(8,128)(2,1)S(1)} copy-done((bf16[256,1,256]{2,0,1:T(8,128)(2,1)S(1)}, bf16[256,1,256]{2,0,1:T(8,128)(2,1)}, u32[]{:S(2)}) %copy-start.1) | copy-done | bytes 131096
  9.1 2.2 %prep.1 = (s32[64]{0:T(128)S(1)}, bf16[4224,256]{1,0:T(8,128)(2,1)S(1)}, f32[4224,128]{1,0:T(8,128)S(1)}, f32[4224,128]{1,0:T(8,128)S(1)}, f32[4224,128]{1,0:T(8,128)S(1)}) custom-call(s32[6]{0:T(128)S(1)} %pad_add_fusion.meta_ref, bf16[256,1024]{1,0:T(8,128)(2,1)S(1)} %copy-done, bf16[256,1024]{1,0:T(8,128)(2,1)S(1)} %collective-permute-done.4.far_ref, ...), custom_call_target="tpu_custom_call" | custom-call | flops 268435456 | bytes 3145728 | tf_op jit(solution)/shard_map/prep/pallas_call | solution.py:130
  11.3 0.0 collective-permute-done.2
  11.3 0.0 collective-permute-done.1
  11.3 0.0 collective-permute-done
  11.4 0.4 collective-permute-start.9
  11.8 0.5 collective-permute-start.8
  12.2 1.1 %collective-permute-start.7 = (bf16[1024,256]{1,0:T(8,128)(2,1)S(1)}, bf16[1024,256]{1,0:T(8,128)(2,1)S(1)}, u32[]{:S(2)}, u32[]{:S(2)}) collective-permute-start(bf16[1024,256]{1,0:T(8,128)(2,1)S(1)} %constant_dynamic-update-slice_fusion), channel_id=1, source_target_pairs={{0,64},{16,48},{64,0},{80,112},{128,192},{144,176},{192,128},{208,... | collective-permute-start | bytes 1572872 | tf_op jit(solution)/shard_map/ppermute | solution.py:311
  13.3 1.2 %collective-permute-start.6 = (bf16[1024,256]{1,0:T(8,128)(2,1)S(1)}, bf16[1024,256]{1,0:T(8,128)(2,1)S(1)}, u32[]{:S(2)}, u32[]{:S(2)}) collective-permute-start(bf16[1024,256]{1,0:T(8,128)(2,1)S(1)} %constant_dynamic-update-slice_fusion.2), channel_id=1, source_target_pairs={{0,192},{16,49},{64,128},{80,113},{128,64},{144,177},{192,0},{208,... | collective-permute-start | bytes 1572872 | tf_op jit(solution)/shard_map/ppermute | solution.py:312
  14.5 0.1 pad_maximum_fusion.refs_2_
  14.6 1.1 %collective-permute-start.5 = (bf16[2048,256]{1,0:T(8,128)(2,1)S(1)}, bf16[2048,256]{1,0:T(8,128)(2,1)S(1)}, u32[]{:S(2)}, u32[]{:S(2)}) collective-permute-start(bf16[2048,256]{1,0:T(8,128)(2,1)S(1)} %pad_maximum_fusion.refs_2_), channel_id=1, source_target_pairs={{0,128},{16,17},{64,192},{80,81},{128,0},{144,145},{192,64},{208,2... | collective-permute-start | bytes 3145736 | tf_op jit(solution)/shard_map/ppermute | solution.py:314
  15.7 10.5 %fold0.1 = (f32[4224,128]{1,0:T(8,128)S(1)}, f32[4224,128]{1,0:T(8,128)S(1)}, f32[4224,128]{1,0:T(8,128)S(1)}) custom-call(s32[64]{0:T(128)S(1)} %get-tuple-element.52.refs_0_, bf16[4224,256]{1,0:T(8,128)(2,1)S(1)} %get-tuple-element.53.refs_1_, ...), custom_call_target="tpu_custom_call", output_to_operand_aliasing={{0}: (3, {}), {1}: (4, {}), {2}: (5, {})} | custom-call | flops 2684354560 | bytes 4194304 | tf_op jit(solution)/shard_map/fold0/pallas_call | solution.py:245
  26.2 0.0 collective-permute-done.9
  26.2 0.0 collective-permute-done.8
  26.2 0.1 pad_maximum_fusion.1.refs_2_
  26.3 7.7 %fold1.1 = (f32[4224,128]{1,0:T(8,128)S(1)}, f32[4224,128]{1,0:T(8,128)S(1)}, f32[4224,128]{1,0:T(8,128)S(1)}) custom-call(s32[64]{0:T(128)S(1)} %get-tuple-element.52.refs_0_, bf16[4224,256]{1,0:T(8,128)(2,1)S(1)} %get-tuple-element.53.refs_1_, ...), custom_call_target="tpu_custom_call", output_to_operand_aliasing={{0}: (3, {}), {1}: (4, {}), {2}: (5, {})} | custom-call | flops 2684354560 | bytes 4194304 | tf_op jit(solution)/shard_map/fold1/pallas_call | solution.py:245
  33.9 0.0 collective-permute-done.7
  33.9 0.0 collective-permute-done.6
  34.0 0.1 pad_maximum_fusion.2.refs_2_
  34.0 7.5 %fold2.1 = (f32[4224,128]{1,0:T(8,128)S(1)}, f32[4224,128]{1,0:T(8,128)S(1)}, f32[4224,128]{1,0:T(8,128)S(1)}) custom-call(s32[64]{0:T(128)S(1)} %get-tuple-element.52.refs_0_, bf16[4224,256]{1,0:T(8,128)(2,1)S(1)} %get-tuple-element.53.refs_1_, ...), custom_call_target="tpu_custom_call", output_to_operand_aliasing={{0}: (3, {}), {1}: (4, {}), {2}: (5, {})} | custom-call | flops 2684354560 | bytes 4194304 | tf_op jit(solution)/shard_map/fold2/pallas_call | solution.py:245
  41.5 0.0 collective-permute-done.5.refs_2_
  41.5 0.0 copy-start.2
  41.5 4.5 %fold3.1 = (f32[4224,128]{1,0:T(8,128)S(1)}, f32[4224,128]{1,0:T(8,128)S(1)}, f32[4224,128]{1,0:T(8,128)S(1)}, bf16[256,1024]{1,0:T(8,128)(2,1)S(1)}, f32[256,128]{1,0:T(8,128)S(1)}) custom-call(s32[64]{0:T(128)S(1)} %get-tuple-element.52.refs_0_, ...), custom_call_target="tpu_custom_call", output_to_operand_aliasing={{0}: (3, {}), {1}: (4, {}), {2}: (5, {})} | custom-call | flops 2684354560 | bytes 4194304 | tf_op jit(solution)/shard_map/fold3/pallas_call | solution.py:245
  46.0 3.9 %collective-permute-start.10 = (bf16[256,1024]{1,0:T(8,128)(2,1)S(1)}, bf16[256,1024]{1,0:T(8,128)(2,1)S(1)}, u32[]{:S(2)}, u32[]{:S(2)}) collective-permute-start(bf16[256,1024]{1,0:T(8,128)(2,1)S(1)} %get-tuple-element.87), channel_id=1, source_target_pairs={{0,16},{16,0},{64,80},{80,64},{128,144},{144,128},{192,208},{208,1... | collective-permute-start | bytes 1572872 | tf_op jit(solution)/shard_map/ppermute | solution.py:322
  49.9 0.1 collective-permute-start.11
  50.0 1.6 %collective-permute-done.11.far_stat_ref = f32[256,128]{1,0:T(8,128)S(1)} collective-permute-done((f32[256,128]{1,0:T(8,128)S(1)}, f32[256,128]{1,0:T(8,128)S(1)}, u32[]{:S(2)}, u32[]{:S(2)}) %collective-permute-start.11) | collective-permute-done | bytes 131104 | tf_op jit(solution)/shard_map/ppermute | solution.py:323
  51.7 0.0 collective-permute-done.10.far_ref
  51.7 0.0 copy-done.2
  51.7 2.5 %join.1 = bf16[256,1024]{1,0:T(8,128)(2,1)} custom-call(s32[2]{0:T(128)S(1)} %copy-done.2, f32[4224,128]{1,0:T(8,128)S(1)} %get-tuple-element.84.m_ref, f32[4224,128]{1,0:T(8,128)S(1)} %get-tuple-element.85.l_ref, f32[4224,128]{1,0:T(8,128)S(1)} %get-tuple-element.86.a_ref, bf16[256,1024]{1,0:T(8,128)(2,1)S(1)} %collective-permute-done.10.far_ref, ...), custom_call_target="tpu_custom_call" | custom-call | tf_op jit(solution)/shard_map/join/pallas_call | solution.py:289
  (3 shorter events, 0.1 us)
Async XLA Ops:
  0.0 7.1 %collective-permute-start.4 = (bf16[256,1024]{1,0:T(8,128)(2,1)}, bf16[256,1024]{1,0:T(8,128)(2,1)S(1)}, u32[]{:S(2)}, u32[]{:S(2)}) collective-permute-start(bf16[256,1024]{1,0:T(8,128)(2,1)} %q_ref.1), channel_id=1, source_target_pairs={{0,16},{16,0},{64,80},{80,64},{128,144},{144,128},{192,208},{208,1... | collective-permute-start | bytes 1572872 | tf_op jit(solution)/shard_map/ppermute | solution.py:306
  0.7 10.6 %collective-permute-start.2 = (bf16[512,256]{1,0:T(8,128)(2,1)}, bf16[512,256]{1,0:T(8,128)(2,1)S(1)}, u32[]{:S(2)}, u32[]{:S(2)}) collective-permute-start(bf16[512,256]{1,0:T(8,128)(2,1)} %bitcast.7), channel_id=1, source_target_pairs={{0,1},{16,144},{64,65},{80,208},{128,129},{144,16},{192,193},{208,... | collective-permute-start | bytes 786440 | tf_op jit(solution)/shard_map/ppermute | solution.py:305
  2.7 8.6 %collective-permute-start.1 = (bf16[512,256]{1,0:T(8,128)(2,1)}, bf16[512,256]{1,0:T(8,128)(2,1)S(1)}, u32[]{:S(2)}, u32[]{:S(2)}) collective-permute-start(bf16[512,256]{1,0:T(8,128)(2,1)} %bitcast.8), channel_id=1, source_target_pairs={{0,33},{16,208},{64,97},{80,144},{128,161},{144,80},{192,225},{208... | collective-permute-start | bytes 786440 | tf_op jit(solution)/shard_map/ppermute | solution.py:305
  2.7 8.6 %collective-permute-start = (bf16[512,256]{1,0:T(8,128)(2,1)}, bf16[512,256]{1,0:T(8,128)(2,1)S(1)}, u32[]{:S(2)}, u32[]{:S(2)}) collective-permute-start(bf16[512,256]{1,0:T(8,128)(2,1)} %bitcast.9), channel_id=1, source_target_pairs={{0,32},{16,80},{64,96},{80,16},{128,160},{144,208},{192,224},{208,... | collective-permute-start | bytes 786440 | tf_op jit(solution)/shard_map/ppermute | solution.py:305
  5.2 1.8 %collective-permute-start.3 = (s32[2]{0:T(128)S(1)}, s32[2]{0:T(128)S(1)}, u32[]{:S(2)}, u32[]{:S(2)}) collective-permute-start(s32[2]{0:T(128)S(1)} %bitcast_add_fusion), channel_id=1, source_target_pairs={{0,16},{16,0},{64,80},{80,64},{128,144},{144,128},{192,208},{208,1... | collective-permute-start | bytes 32 | tf_op jit(solution)/shard_map/ppermute | solution.py:306
  7.1 1.0 %copy-start = (bf16[256,1024]{1,0:T(8,128)(2,1)S(1)}, bf16[256,1024]{1,0:T(8,128)(2,1)}, u32[]{:S(2)}) copy-start(bf16[256,1024]{1,0:T(8,128)(2,1)} %q_ref.1) | copy-start | bytes 1572868
  8.2 0.9 %copy-start.1 = (bf16[256,1,256]{2,0,1:T(8,128)(2,1)S(1)}, bf16[256,1,256]{2,0,1:T(8,128)(2,1)}, u32[]{:S(2)}) copy-start(bf16[256,1,256]{2,0,1:T(8,128)(2,1)} %param.6) | copy-start | bytes 393220
  11.4 14.8 %collective-permute-start.9 = (bf16[1024,256]{1,0:T(8,128)(2,1)S(1)}, bf16[1024,256]{1,0:T(8,128)(2,1)S(1)}, u32[]{:S(2)}, u32[]{:S(2)}) collective-permute-start(bf16[1024,256]{1,0:T(8,128)(2,1)S(1)} %constant_dynamic-update-slice_fusion), channel_id=1, source_target_pairs={{0,192},{16,49},{64,128},{80,113},{128,64},{144,177},{192,0},{208,... | collective-permute-start | bytes 1572872 | tf_op jit(solution)/shard_map/ppermute | solution.py:312
  11.8 14.4 %collective-permute-start.8 = (bf16[1024,256]{1,0:T(8,128)(2,1)S(1)}, bf16[1024,256]{1,0:T(8,128)(2,1)S(1)}, u32[]{:S(2)}, u32[]{:S(2)}) collective-permute-start(bf16[1024,256]{1,0:T(8,128)(2,1)S(1)} %constant_dynamic-update-slice_fusion.2), channel_id=1, source_target_pairs={{0,64},{16,48},{64,0},{80,112},{128,192},{144,176},{192,128},{208,... | collective-permute-start | bytes 1572872 | tf_op jit(solution)/shard_map/ppermute | solution.py:311
  12.2 21.7 %collective-permute-start.7 = (bf16[1024,256]{1,0:T(8,128)(2,1)S(1)}, bf16[1024,256]{1,0:T(8,128)(2,1)S(1)}, u32[]{:S(2)}, u32[]{:S(2)}) collective-permute-start(bf16[1024,256]{1,0:T(8,128)(2,1)S(1)} %constant_dynamic-update-slice_fusion), channel_id=1, source_target_pairs={{0,64},{16,48},{64,0},{80,112},{128,192},{144,176},{192,128},{208,... | collective-permute-start | bytes 1572872 | tf_op jit(solution)/shard_map/ppermute | solution.py:311
  13.3 20.6 %collective-permute-start.6 = (bf16[1024,256]{1,0:T(8,128)(2,1)S(1)}, bf16[1024,256]{1,0:T(8,128)(2,1)S(1)}, u32[]{:S(2)}, u32[]{:S(2)}) collective-permute-start(bf16[1024,256]{1,0:T(8,128)(2,1)S(1)} %constant_dynamic-update-slice_fusion.2), channel_id=1, source_target_pairs={{0,192},{16,49},{64,128},{80,113},{128,64},{144,177},{192,0},{208,... | collective-permute-start | bytes 1572872 | tf_op jit(solution)/shard_map/ppermute | solution.py:312
  14.6 26.9 %collective-permute-start.5 = (bf16[2048,256]{1,0:T(8,128)(2,1)S(1)}, bf16[2048,256]{1,0:T(8,128)(2,1)S(1)}, u32[]{:S(2)}, u32[]{:S(2)}) collective-permute-start(bf16[2048,256]{1,0:T(8,128)(2,1)S(1)} %pad_maximum_fusion.refs_2_), channel_id=1, source_target_pairs={{0,128},{16,17},{64,192},{80,81},{128,0},{144,145},{192,64},{208,2... | collective-permute-start | bytes 3145736 | tf_op jit(solution)/shard_map/ppermute | solution.py:314
  41.5 10.1 %copy-start.2 = (s32[2]{0:T(128)S(1)}, s32[2]{0:T(128)}, u32[]{:S(2)}) copy-start(s32[2]{0:T(128)} %len_ref.1) | copy-start | bytes 28
  46.0 5.6 %collective-permute-start.10 = (bf16[256,1024]{1,0:T(8,128)(2,1)S(1)}, bf16[256,1024]{1,0:T(8,128)(2,1)S(1)}, u32[]{:S(2)}, u32[]{:S(2)}) collective-permute-start(bf16[256,1024]{1,0:T(8,128)(2,1)S(1)} %get-tuple-element.87), channel_id=1, source_target_pairs={{0,16},{16,0},{64,80},{80,64},{128,144},{144,128},{192,208},{208,1... | collective-permute-start | bytes 1572872 | tf_op jit(solution)/shard_map/ppermute | solution.py:322
  49.9 1.7 %collective-permute-start.11 = (f32[256,128]{1,0:T(8,128)S(1)}, f32[256,128]{1,0:T(8,128)S(1)}, u32[]{:S(2)}, u32[]{:S(2)}) collective-permute-start(f32[256,128]{1,0:T(8,128)S(1)} %get-tuple-element.88), channel_id=1, source_target_pairs={{0,16},{16,0},{64,80},{80,64},{128,144},{144,128},{192,208},{208,1... | collective-permute-start | bytes 393224 | tf_op jit(solution)/shard_map/ppermute | solution.py:323
where the time goes:
time: 54.9 us; the launch traced here: 54.2 us
  Pallas kernels  34.9 us (64%)
  starting transfers between devices  13.6 us (25%)
  local copies, waits for them, and re-layouts  3 us (5%)
  waiting for transfers between devices  1.65 us (3%)
  other arithmetic  0.96 us (2%)
    pallas_call x4, Pallas kernels, fold_call(): pl.pallas_call(functools.partial(fold_kernel, number), out_shape=[jax.Sha...  30.1 us
    ppermute x1, starting transfers between devices, per_device(): far = lax.ppermute(far, AXES, core_swap())  3.9 us
    ppermute x3, starting transfers between devices, per_device(): lax.ppermute(piece, AXES, ring_swap(0, turn))  3.86 us
    pallas_call x1, Pallas kernels, join(): pl.pallas_call(join_kernel, out_shape=jax.ShapeDtypeStruct((256, 1024), j...  2.53 us
    pallas_call x1, Pallas kernels, prep(): pl.pallas_call(prep_kernel, out_shape=[jax.ShapeDtypeStruct((64,), jnp.in...  2.2 us
    unnamed x7, local copies, waits for them, and re-layouts  1.97 us
    ppermute x1, waiting for transfers between devices, per_device(): far_stat = lax.ppermute(far_stat, AXES, core_swap())  1.62 us
    ppermute x2, starting transfers between devices, per_device(): even0, even1 = [lax.ppermute(h, AXES, ring_swap(1, 'even')) for h in held]  1.55 us
  transfers between devices with their start and end apart: 12, of which 1 were waited for; matrix products, arithmetic and copies ran while one was open for 4% of the time, Pallas kernels for 51%

commit v1 on v0

--- a/solution.py
+++ b/solution.py
@@ -70,7 +70,7 @@
     offset = jnp.int32(0)
     for want in range(2):
         count = jnp.int32(0)
-        for b in range(4):
+        for b in (2, 3, 0, 1):
             code = meta_ref[b]
             live = ((code & 255) + (GROUP - 1)) // GROUP
             live = jnp.where((code >> 8) == (meta_ref[4] ^ want), live, 0)
@@ -81,6 +81,8 @@
 
             lax.fori_loop(0, live, add, 0)
             count = count + live
+            if b == 3:
+                plan_ref[3 + want] = (count + (TILE - 1)) // TILE
         tiles = (count + (TILE - 1)) // TILE
         for i in range(TILE - 1):
             plan_ref[LIST + offset + count + i] = SPARE
@@ -151,7 +153,9 @@
 
     items, first = jnp.int32(0), jnp.int32(LIST)
     for want in range(2):
-        tiles = plan_ref[want]
+        tiles, far_tiles = plan_ref[want], plan_ref[3 + want]
+        start = far_tiles if number == 4 else 0
+        used = (far_tiles if number == 3 else tiles) - start
         if number == 1:
             blocks, many = (want, 0), 1
         elif number == 2:
@@ -160,18 +164,18 @@
             blocks = (jnp.where(core == 0, want, 0), 1)
             many = jnp.where(core == 0, 1, 2 if (want == 0) == (number == 0) else 0)
 
-        def add(t, c, first=first, blocks=blocks, many=many, items=items):
+        def add(t, c, first=first, blocks=blocks, many=many, items=items, start=start):
             for i in range(1 if number in (1, 2) else 2):
 
                 @pl.when(i < many)
                 def _(i=i):
-                    item_at[items + t * many + i] = first + t * TILE
+                    item_at[items + t * many + i] = first + (start + t) * TILE
                     item_kv[items + t * many + i] = blocks[i]
 
             return c
 
-        lax.fori_loop(0, tiles, add, 0)
-        items = items + tiles * many
+        lax.fori_loop(0, used, add, 0)
+        items = items + used * many
         first = first + tiles * TILE
     for i in range(2):
         item_at[items + i] = LIST
@@ -321,6 +325,7 @@
     *state, far, far_stat = fold_call(3, plan, qs, across, state)
     far = lax.ppermute(far, AXES, core_swap())
     far_stat = lax.ppermute(far_stat, AXES, core_swap())
+    state = fold_call(4, plan, qs, across, state)
     return join(answer_len, state, far, far_stat)
 
 

time: 54.9 us -> 55.7 us (1.015)
  the two profiles are of different devices: /device:TPU:141 before, /device:TPU:1 now
where the time goes in v1:
time: 55.7 us; the launch traced here: 55.9 us
  Pallas kernels  32 us (57%)
  starting transfers between devices  12.1 us (22%)
  waiting for transfers between devices  7.66 us (14%)
  local copies, waits for them, and re-layouts  2.99 us (5%)
  other arithmetic  0.96 us (2%)
    pallas_call x5, Pallas kernels, fold_call(): pl.pallas_call(functools.partial(fold_kernel, number), out_shape=[jax.Sha...  27.6 us
    ppermute x1, waiting for transfers between devices, per_device(): across = lax.ppermute(all_held, AXES, ring_swap(1, 'across'))  4.91 us
    ppermute x2, starting transfers between devices, per_device(): lax.ppermute(v, AXES, core_swap())  4.08 us
    ppermute x2, starting transfers between devices, per_device(): odd0, odd1 = [lax.ppermute(h, AXES, ring_swap(1, 'odd')) for h in held]  2.76 us
    ppermute x3, starting transfers between devices, per_device(): lax.ppermute(piece, AXES, ring_swap(0, turn))  2.65 us
    pallas_call x1, Pallas kernels, join(): pl.pallas_call(join_kernel, out_shape=jax.ShapeDtypeStruct((256, 1024), j...  2.25 us
    pallas_call x1, Pallas kernels, prep(): pl.pallas_call(prep_kernel, out_shape=[jax.ShapeDtypeStruct((64,), jnp.in...  2.19 us
    ppermute x2, waiting for transfers between devices, per_device(): odd0, odd1 = [lax.ppermute(h, AXES, ring_swap(1, 'odd')) for h in held]  2.09 us
  transfers between devices with their start and end apart: 12, of which 3 were waited for; matrix products, arithmetic and copies ran while one was open for 4% of the time, Pallas kernels for 40%

profile of v1, /device:TPU:1, one launch (start us, length us, event | category | flops | bytes accessed | tf_op | source)
XLA Modules:
  0.0 55.9 jit_solution(17998029713515265450)
XLA Ops:
  0.0 3.2 %collective-permute-start.4 = (bf16[256,1024]{1,0:T(8,128)(2,1)}, bf16[256,1024]{1,0:T(8,128)(2,1)S(1)}, u32[]{:S(2)}, u32[]{:S(2)}) collective-permute-start(bf16[256,1024]{1,0:T(8,128)(2,1)} %q_ref.1), channel_id=1, source_target_pairs={{0,16},{16,0},{64,80},{80,64},{128,144},{144,128},{192,208},{208,1... | collective-permute-start | bytes 1572872 | tf_op jit(solution)/shard_map/ppermute | solution.py:310
  3.2 1.2 %collective-permute-start.2 = (bf16[512,256]{1,0:T(8,128)(2,1)}, bf16[512,256]{1,0:T(8,128)(2,1)S(1)}, u32[]{:S(2)}, u32[]{:S(2)}) collective-permute-start(bf16[512,256]{1,0:T(8,128)(2,1)} %bitcast.7), channel_id=1, source_target_pairs={{0,1},{16,144},{64,65},{80,208},{128,129},{144,16},{192,193},{208,... | collective-permute-start | bytes 786440 | tf_op jit(solution)/shard_map/ppermute | solution.py:309
  4.4 0.8 %collective-permute-start.1 = (bf16[512,256]{1,0:T(8,128)(2,1)}, bf16[512,256]{1,0:T(8,128)(2,1)S(1)}, u32[]{:S(2)}, u32[]{:S(2)}) collective-permute-start(bf16[512,256]{1,0:T(8,128)(2,1)} %bitcast.8), channel_id=1, source_target_pairs={{0,33},{16,208},{64,97},{80,144},{128,161},{144,80},{192,225},{208... | collective-permute-start | bytes 786440 | tf_op jit(solution)/shard_map/ppermute | solution.py:309
  5.2 0.7 %collective-permute-start = (bf16[512,256]{1,0:T(8,128)(2,1)}, bf16[512,256]{1,0:T(8,128)(2,1)S(1)}, u32[]{:S(2)}, u32[]{:S(2)}) collective-permute-start(bf16[512,256]{1,0:T(8,128)(2,1)} %bitcast.9), channel_id=1, source_target_pairs={{0,32},{16,80},{64,96},{80,16},{128,160},{144,208},{192,224},{208,... | collective-permute-start | bytes 786440 | tf_op jit(solution)/shard_map/ppermute | solution.py:309
  5.9 0.7 %bitcast_add_fusion = s32[2]{0:T(128)S(1)} fusion(s32[2]{0:T(128)} %len_ref.1, s32[2,1]{0,1:T(1,128)} %param.8), kind=kLoop, calls=%fused_computation.6 | loop fusion | flops 4 | bytes 24 | tf_op jit(solution)/shard_map/add | solution.py:306
  6.6 0.8 %collective-permute-start.3 = (s32[2]{0:T(128)S(1)}, s32[2]{0:T(128)S(1)}, u32[]{:S(2)}, u32[]{:S(2)}) collective-permute-start(s32[2]{0:T(128)S(1)} %bitcast_add_fusion), channel_id=1, source_target_pairs={{0,16},{16,0},{64,80},{80,64},{128,144},{144,128},{192,208},{208,1... | collective-permute-start | bytes 32 | tf_op jit(solution)/shard_map/ppermute | solution.py:310
  7.4 1.0 %pad.4 = bf16[1024,256]{1,0:T(8,128)(2,1)S(1)} pad(bf16[512,256]{1,0:T(8,128)(2,1)} %bitcast.10, bf16[]{:T(256)} %constant.4.clone.1), padding=0_512x0_0 | pad | bytes 786434 | tf_op jit(solution)/shard_map/jit(_pad)/pad | solution.py:311
  8.4 0.0 collective-permute-done.3
  8.4 0.1 pad_add_fusion.meta_ref
  8.5 0.0 collective-permute-done.4.far_ref
  8.5 0.0 copy-start
  8.5 1.0 %copy-done = bf16[256,1024]{1,0:T(8,128)(2,1)S(1)} copy-done((bf16[256,1024]{1,0:T(8,128)(2,1)S(1)}, bf16[256,1024]{1,0:T(8,128)(2,1)}, u32[]{:S(2)}) %copy-start) | copy-done | bytes 524312
  9.5 0.0 copy-start.1
  9.5 0.9 %copy-done.1 = bf16[256,1,256]{2,0,1:T(8,128)(2,1)S(1)} copy-done((bf16[256,1,256]{2,0,1:T(8,128)(2,1)S(1)}, bf16[256,1,256]{2,0,1:T(8,128)(2,1)}, u32[]{:S(2)}) %copy-start.1) | copy-done | bytes 131096
  10.4 2.2 %prep.1 = (s32[64]{0:T(128)S(1)}, bf16[4224,256]{1,0:T(8,128)(2,1)S(1)}, f32[4224,128]{1,0:T(8,128)S(1)}, f32[4224,128]{1,0:T(8,128)S(1)}, f32[4224,128]{1,0:T(8,128)S(1)}) custom-call(s32[6]{0:T(128)S(1)} %pad_add_fusion.meta_ref, bf16[256,1024]{1,0:T(8,128)(2,1)S(1)} %copy-done, bf16[256,1024]{1,0:T(8,128)(2,1)S(1)} %collective-permute-done.4.far_ref, ...), custom_call_target="tpu_custom_call" | custom-call | flops 268435456 | bytes 3145728 | tf_op jit(solution)/shard_map/prep/pallas_call | solution.py:132
  12.6 0.0 collective-permute-done.2
  12.7 0.6 %collective-permute-done.1 = bf16[512,256]{1,0:T(8,128)(2,1)S(1)} collective-permute-done((bf16[512,256]{1,0:T(8,128)(2,1)}, bf16[512,256]{1,0:T(8,128)(2,1)S(1)}, u32[]{:S(2)}, u32[]{:S(2)}) %collective-permute-start.1) | collective-permute-done | bytes 262176 | tf_op jit(solution)/shard_map/ppermute | solution.py:309
  13.3 0.0 collective-permute-done
  13.3 1.2 %collective-permute-start.9 = (bf16[1024,256]{1,0:T(8,128)(2,1)S(1)}, bf16[1024,256]{1,0:T(8,128)(2,1)S(1)}, u32[]{:S(2)}, u32[]{:S(2)}) collective-permute-start(bf16[1024,256]{1,0:T(8,128)(2,1)S(1)} %constant_dynamic-update-slice_fusion), channel_id=1, source_target_pairs={{0,192},{16,49},{64,128},{80,113},{128,64},{144,177},{192,0},{208,... | collective-permute-start | bytes 1572872 | tf_op jit(solution)/shard_map/ppermute | solution.py:316
  14.6 0.2 collective-permute-start.8
  14.8 1.3 %collective-permute-start.7 = (bf16[1024,256]{1,0:T(8,128)(2,1)S(1)}, bf16[1024,256]{1,0:T(8,128)(2,1)S(1)}, u32[]{:S(2)}, u32[]{:S(2)}) collective-permute-start(bf16[1024,256]{1,0:T(8,128)(2,1)S(1)} %constant_dynamic-update-slice_fusion), channel_id=1, source_target_pairs={{0,64},{16,48},{64,0},{80,112},{128,192},{144,176},{192,128},{208,... | collective-permute-start | bytes 1572872 | tf_op jit(solution)/shard_map/ppermute | solution.py:315
  16.1 1.6 %collective-permute-start.6 = (bf16[1024,256]{1,0:T(8,128)(2,1)S(1)}, bf16[1024,256]{1,0:T(8,128)(2,1)S(1)}, u32[]{:S(2)}, u32[]{:S(2)}) collective-permute-start(bf16[1024,256]{1,0:T(8,128)(2,1)S(1)} %constant_dynamic-update-slice_fusion.2), channel_id=1, source_target_pairs={{0,192},{16,49},{64,128},{80,113},{128,64},{144,177},{192,0},{208,... | collective-permute-start | bytes 1572872 | tf_op jit(solution)/shard_map/ppermute | solution.py:316
  17.7 0.1 pad_maximum_fusion.refs_2_
  17.7 0.5 collective-permute-start.5
  18.2 2.7 %fold0.1 = (f32[4224,128]{1,0:T(8,128)S(1)}, f32[4224,128]{1,0:T(8,128)S(1)}, f32[4224,128]{1,0:T(8,128)S(1)}) custom-call(s32[64]{0:T(128)S(1)} %get-tuple-element.55.refs_0_, bf16[4224,256]{1,0:T(8,128)(2,1)S(1)} %get-tuple-element.56.refs_1_, ...), custom_call_target="tpu_custom_call", output_to_operand_aliasing={{0}: (3, {}), {1}: (4, {}), {2}: (5, {})} | custom-call | flops 2684354560 | bytes 4194304 | tf_op jit(solution)/shard_map/fold0/pallas_call | solution.py:249
  20.9 2.1 %collective-permute-done.9 = bf16[1024,256]{1,0:T(8,128)(2,1)S(1)} collective-permute-done((bf16[1024,256]{1,0:T(8,128)(2,1)S(1)}, bf16[1024,256]{1,0:T(8,128)(2,1)S(1)}, u32[]{:S(2)}, u32[]{:S(2)}) %collective-permute-start.9) | collective-permute-done | bytes 524320 | tf_op jit(solution)/shard_map/ppermute | solution.py:316
  23.0 0.0 collective-permute-done.8
  23.0 0.1 pad_maximum_fusion.1.refs_2_
  23.1 6.6 %fold1.1 = (f32[4224,128]{1,0:T(8,128)S(1)}, f32[4224,128]{1,0:T(8,128)S(1)}, f32[4224,128]{1,0:T(8,128)S(1)}) custom-call(s32[64]{0:T(128)S(1)} %get-tuple-element.55.refs_0_, bf16[4224,256]{1,0:T(8,128)(2,1)S(1)} %get-tuple-element.56.refs_1_, ...), custom_call_target="tpu_custom_call", output_to_operand_aliasing={{0}: (3, {}), {1}: (4, {}), {2}: (5, {})} | custom-call | flops 2684354560 | bytes 4194304 | tf_op jit(solution)/shard_map/fold1/pallas_call | solution.py:249
  29.7 0.0 collective-permute-done.7
  29.7 0.0 collective-permute-done.6
  29.7 0.1 pad_maximum_fusion.2.refs_2_
  29.8 6.4 %fold2.1 = (f32[4224,128]{1,0:T(8,128)S(1)}, f32[4224,128]{1,0:T(8,128)S(1)}, f32[4224,128]{1,0:T(8,128)S(1)}) custom-call(s32[64]{0:T(128)S(1)} %get-tuple-element.55.refs_0_, bf16[4224,256]{1,0:T(8,128)(2,1)S(1)} %get-tuple-element.56.refs_1_, ...), custom_call_target="tpu_custom_call", output_to_operand_aliasing={{0}: (3, {}), {1}: (4, {}), {2}: (5, {})} | custom-call | flops 2684354560 | bytes 4194304 | tf_op jit(solution)/shard_map/fold2/pallas_call | solution.py:249
  36.2 4.9 %collective-permute-done.5.refs_2_ = bf16[2048,256]{1,0:T(8,128)(2,1)S(1)} collective-permute-done((bf16[2048,256]{1,0:T(8,128)(2,1)S(1)}, bf16[2048,256]{1,0:T(8,128)(2,1)S(1)}, u32[]{:S(2)}, u32[]{:S(2)}) %collective-permute-start.5) | collective-permute-done | bytes 1048608 | tf_op jit(solution)/shard_map/ppermute | solution.py:318
  41.1 7.7 %fold3.1 = (f32[4224,128]{1,0:T(8,128)S(1)}, f32[4224,128]{1,0:T(8,128)S(1)}, f32[4224,128]{1,0:T(8,128)S(1)}, bf16[256,1024]{1,0:T(8,128)(2,1)S(1)}, f32[256,128]{1,0:T(8,128)S(1)}) custom-call(s32[64]{0:T(128)S(1)} %get-tuple-element.55.refs_0_, ...), custom_call_target="tpu_custom_call", output_to_operand_aliasing={{0}: (3, {}), {1}: (4, {}), {2}: (5, {})} | custom-call | flops 2684354560 | bytes 4194304 | tf_op jit(solution)/shard_map/fold3/pallas_call | solution.py:249
  48.8 0.1 collective-permute-start.10
  48.9 0.5 collective-permute-start.11
  49.4 0.0 copy-start.2
  49.4 4.3 %fold4.1 = (f32[4224,128]{1,0:T(8,128)S(1)}, f32[4224,128]{1,0:T(8,128)S(1)}, f32[4224,128]{1,0:T(8,128)S(1)}) custom-call(s32[64]{0:T(128)S(1)} %get-tuple-element.55.refs_0_, bf16[4224,256]{1,0:T(8,128)(2,1)S(1)} %get-tuple-element.56.refs_1_, ...), custom_call_target="tpu_custom_call", output_to_operand_aliasing={{0}: (3, {}), {1}: (4, {}), {2}: (5, {})} | custom-call | flops 2684354560 | bytes 4194304 | tf_op jit(solution)/shard_map/fold4/pallas_call | solution.py:249
  53.6 0.0 collective-permute-done.11.far_stat_ref
  53.6 0.0 collective-permute-done.10.far_ref
  53.6 0.0 copy-done.2
  53.6 2.2 %join.1 = bf16[256,1024]{1,0:T(8,128)(2,1)} custom-call(s32[2]{0:T(128)S(1)} %copy-done.2, f32[4224,128]{1,0:T(8,128)S(1)} %get-tuple-element.90.m_ref, f32[4224,128]{1,0:T(8,128)S(1)} %get-tuple-element.91.l_ref, f32[4224,128]{1,0:T(8,128)S(1)} %get-tuple-element.92.a_ref, bf16[256,1024]{1,0:T(8,128)(2,1)S(1)} %collective-permute-done.10.far_ref, ...), custom_call_target="tpu_custom_call" | custom-call | tf_op jit(solution)/shard_map/join/pallas_call | solution.py:293
  (3 shorter events, 0.1 us)
Async XLA Ops:
  0.0 8.5 %collective-permute-start.4 = (bf16[256,1024]{1,0:T(8,128)(2,1)}, bf16[256,1024]{1,0:T(8,128)(2,1)S(1)}, u32[]{:S(2)}, u32[]{:S(2)}) collective-permute-start(bf16[256,1024]{1,0:T(8,128)(2,1)} %q_ref.1), channel_id=1, source_target_pairs={{0,16},{16,0},{64,80},{80,64},{128,144},{144,128},{192,208},{208,1... | collective-permute-start | bytes 1572872 | tf_op jit(solution)/shard_map/ppermute | solution.py:310
  3.2 9.4 %collective-permute-start.2 = (bf16[512,256]{1,0:T(8,128)(2,1)}, bf16[512,256]{1,0:T(8,128)(2,1)S(1)}, u32[]{:S(2)}, u32[]{:S(2)}) collective-permute-start(bf16[512,256]{1,0:T(8,128)(2,1)} %bitcast.7), channel_id=1, source_target_pairs={{0,1},{16,144},{64,65},{80,208},{128,129},{144,16},{192,193},{208,... | collective-permute-start | bytes 786440 | tf_op jit(solution)/shard_map/ppermute | solution.py:309
  4.4 8.9 %collective-permute-start.1 = (bf16[512,256]{1,0:T(8,128)(2,1)}, bf16[512,256]{1,0:T(8,128)(2,1)S(1)}, u32[]{:S(2)}, u32[]{:S(2)}) collective-permute-start(bf16[512,256]{1,0:T(8,128)(2,1)} %bitcast.8), channel_id=1, source_target_pairs={{0,33},{16,208},{64,97},{80,144},{128,161},{144,80},{192,225},{208... | collective-permute-start | bytes 786440 | tf_op jit(solution)/shard_map/ppermute | solution.py:309
  5.2 8.1 %collective-permute-start = (bf16[512,256]{1,0:T(8,128)(2,1)}, bf16[512,256]{1,0:T(8,128)(2,1)S(1)}, u32[]{:S(2)}, u32[]{:S(2)}) collective-permute-start(bf16[512,256]{1,0:T(8,128)(2,1)} %bitcast.9), channel_id=1, source_target_pairs={{0,32},{16,80},{64,96},{80,16},{128,160},{144,208},{192,224},{208,... | collective-permute-start | bytes 786440 | tf_op jit(solution)/shard_map/ppermute | solution.py:309
  6.6 1.8 %collective-permute-start.3 = (s32[2]{0:T(128)S(1)}, s32[2]{0:T(128)S(1)}, u32[]{:S(2)}, u32[]{:S(2)}) collective-permute-start(s32[2]{0:T(128)S(1)} %bitcast_add_fusion), channel_id=1, source_target_pairs={{0,16},{16,0},{64,80},{80,64},{128,144},{144,128},{192,208},{208,1... | collective-permute-start | bytes 32 | tf_op jit(solution)/shard_map/ppermute | solution.py:310
  8.5 1.0 %copy-start = (bf16[256,1024]{1,0:T(8,128)(2,1)S(1)}, bf16[256,1024]{1,0:T(8,128)(2,1)}, u32[]{:S(2)}) copy-start(bf16[256,1024]{1,0:T(8,128)(2,1)} %q_ref.1) | copy-start | bytes 1572868
  9.5 0.9 %copy-start.1 = (bf16[256,1,256]{2,0,1:T(8,128)(2,1)S(1)}, bf16[256,1,256]{2,0,1:T(8,128)(2,1)}, u32[]{:S(2)}) copy-start(bf16[256,1,256]{2,0,1:T(8,128)(2,1)} %param.6) | copy-start | bytes 393220
  13.3 9.6 %collective-permute-start.9 = (bf16[1024,256]{1,0:T(8,128)(2,1)S(1)}, bf16[1024,256]{1,0:T(8,128)(2,1)S(1)}, u32[]{:S(2)}, u32[]{:S(2)}) collective-permute-start(bf16[1024,256]{1,0:T(8,128)(2,1)S(1)} %constant_dynamic-update-slice_fusion), channel_id=1, source_target_pairs={{0,192},{16,49},{64,128},{80,113},{128,64},{144,177},{192,0},{208,... | collective-permute-start | bytes 1572872 | tf_op jit(solution)/shard_map/ppermute | solution.py:316
  14.6 8.4 %collective-permute-start.8 = (bf16[1024,256]{1,0:T(8,128)(2,1)S(1)}, bf16[1024,256]{1,0:T(8,128)(2,1)S(1)}, u32[]{:S(2)}, u32[]{:S(2)}) collective-permute-start(bf16[1024,256]{1,0:T(8,128)(2,1)S(1)} %constant_dynamic-update-slice_fusion.2), channel_id=1, source_target_pairs={{0,64},{16,48},{64,0},{80,112},{128,192},{144,176},{192,128},{208,... | collective-permute-start | bytes 1572872 | tf_op jit(solution)/shard_map/ppermute | solution.py:315
  14.8 14.9 %collective-permute-start.7 = (bf16[1024,256]{1,0:T(8,128)(2,1)S(1)}, bf16[1024,256]{1,0:T(8,128)(2,1)S(1)}, u32[]{:S(2)}, u32[]{:S(2)}) collective-permute-start(bf16[1024,256]{1,0:T(8,128)(2,1)S(1)} %constant_dynamic-update-slice_fusion), channel_id=1, source_target_pairs={{0,64},{16,48},{64,0},{80,112},{128,192},{144,176},{192,128},{208,... | collective-permute-start | bytes 1572872 | tf_op jit(solution)/shard_map/ppermute | solution.py:315
  16.1 13.6 %collective-permute-start.6 = (bf16[1024,256]{1,0:T(8,128)(2,1)S(1)}, bf16[1024,256]{1,0:T(8,128)(2,1)S(1)}, u32[]{:S(2)}, u32[]{:S(2)}) collective-permute-start(bf16[1024,256]{1,0:T(8,128)(2,1)S(1)} %constant_dynamic-update-slice_fusion.2), channel_id=1, source_target_pairs={{0,192},{16,49},{64,128},{80,113},{128,64},{144,177},{192,0},{208,... | collective-permute-start | bytes 1572872 | tf_op jit(solution)/shard_map/ppermute | solution.py:316
  17.7 23.4 %collective-permute-start.5 = (bf16[2048,256]{1,0:T(8,128)(2,1)S(1)}, bf16[2048,256]{1,0:T(8,128)(2,1)S(1)}, u32[]{:S(2)}, u32[]{:S(2)}) collective-permute-start(bf16[2048,256]{1,0:T(8,128)(2,1)S(1)} %pad_maximum_fusion.refs_2_), channel_id=1, source_target_pairs={{0,128},{16,17},{64,192},{80,81},{128,0},{144,145},{192,64},{208,2... | collective-permute-start | bytes 3145736 | tf_op jit(solution)/shard_map/ppermute | solution.py:318
  48.8 4.9 %collective-permute-start.10 = (bf16[256,1024]{1,0:T(8,128)(2,1)S(1)}, bf16[256,1024]{1,0:T(8,128)(2,1)S(1)}, u32[]{:S(2)}, u32[]{:S(2)}) collective-permute-start(bf16[256,1024]{1,0:T(8,128)(2,1)S(1)} %get-tuple-element.93), channel_id=1, source_target_pairs={{0,16},{16,0},{64,80},{80,64},{128,144},{144,128},{192,208},{208,1... | collective-permute-start | bytes 1572872 | tf_op jit(solution)/shard_map/ppermute | solution.py:326
  48.9 4.8 %collective-permute-start.11 = (f32[256,128]{1,0:T(8,128)S(1)}, f32[256,128]{1,0:T(8,128)S(1)}, u32[]{:S(2)}, u32[]{:S(2)}) collective-permute-start(f32[256,128]{1,0:T(8,128)S(1)} %get-tuple-element.94), channel_id=1, source_target_pairs={{0,16},{16,0},{64,80},{80,64},{128,144},{144,128},{192,208},{208,1... | collective-permute-start | bytes 393224 | tf_op jit(solution)/shard_map/ppermute | solution.py:327
  49.4 4.3 %copy-start.2 = (s32[2]{0:T(128)S(1)}, s32[2]{0:T(128)}, u32[]{:S(2)}) copy-start(s32[2]{0:T(128)} %len_ref.1) | copy-start | bytes 28
